TPU v7x, 256 devices: a whole 4x4x8 slice. The times are simulated.
256 devices in a mesh: row: 16 (over y, x), col: 8 (over z), vox: 2 (over core).
Axes of the slice: x: 4, y: 4, z: 8, core: 2. Of those that a mesh axis runs over, the one named last changes fastest.
Arguments:
- coeffs_r: bfloat16 [32, 16, 64, 2, 1024], P(None, 'row', None, None, 'col'), may hold values from -0.125 to 0.125
- rhs: bfloat16 [32, 16, 64, 1536], P('col', 'row', None, 'vox'), may hold values from -6 to 6
- inverses: bfloat16 [2, 1024, 1024], replicated, may hold values from -0.1875 to 0.1875
Outputs:
- updated: bfloat16 [32, 16, 64, 1536], P('col', 'row', None, 'vox')
All inputs are finite; a program needn't handle non-finite values.
Results may differ from a plain program's by a relative error of at most 0.0049.
Values may be sent and summed in bfloat16 or wider, within the bound.
A program may use at most 64 MiB of HBM per device.

v0:
```python
import jax
import jax.numpy as jnp
from jax import lax
from jax.sharding import PartitionSpec as P


def spread(value, axis, root):
    mine = lax.axis_index(axis) == root
    return lax.psum(jnp.where(mine, value, jnp.zeros_like(value)), axis)


def solve_block(inverse, rhs_block, col_pos, own_cols):
    solved_all = jnp.dot(inverse, rhs_block, preferred_element_type=jnp.float32).astype(
        jnp.bfloat16
    )
    solved_mine = lax.dynamic_slice_in_dim(solved_all, col_pos * own_cols, own_cols, 0)
    return (solved_all, solved_mine)


def local(coeffs_r, rhs, inverses):
    row_count = lax.axis_size("row")
    col_count = lax.axis_size("col")
    row_pos = lax.axis_index("row")
    col_pos = lax.axis_index("col")
    per_col = rhs.shape[0]
    block_rows = rhs.shape[2]
    voxels = rhs.shape[3]
    cycles = coeffs_r.shape[0]
    own_cols = coeffs_r.shape[4]
    block_order = inverses.shape[1]
    tail_cycles = block_order // (block_rows * row_count)
    owner_col = col_count - 1
    tail_piece = rhs[per_col - tail_cycles :]
    tail_rows = lax.all_gather(tail_piece, "row", axis=1, tiled=True)
    tail_rows = spread(tail_rows, "col", owner_col)
    solved_last, last_mine = solve_block(
        inverses[1], tail_rows.reshape(block_order, voxels), col_pos, own_cols
    )
    panel_rows = coeffs_r[cycles - 2 * tail_cycles : cycles - tail_cycles, 0, :, 1, :]
    panel_rows = panel_rows.reshape(tail_cycles * block_rows, own_cols)
    partial_value = -jnp.dot(panel_rows, last_mine, preferred_element_type=jnp.float32)
    known = rhs[per_col - 2 * tail_cycles : per_col - tail_cycles, 0]
    known = known.reshape(tail_cycles * block_rows, voxels).astype(jnp.float32)
    partial_value = partial_value + jnp.where(col_pos == owner_col, known, jnp.zeros_like(known))
    partial_value = partial_value.reshape(tail_cycles, 1, block_rows, voxels)
    padded = jnp.zeros((tail_cycles, row_count, block_rows, voxels), jnp.float32)
    anchor = jnp.zeros((), jnp.int32)
    padded = lax.dynamic_update_slice(padded, partial_value, (anchor, row_pos, anchor, anchor))
    middle_rhs = lax.psum(padded, ("row", "col")).astype(jnp.bfloat16)
    solved_first, first_mine = solve_block(
        inverses[0], middle_rhs.reshape(block_order, voxels), col_pos, own_cols
    )
    stacked_mine = jnp.stack([first_mine, last_mine])
    removed = lax.psum_scatter(
        jnp.einsum("kprjc,jcv->kprv", coeffs_r, stacked_mine, preferred_element_type=jnp.float32),
        "col",
        scatter_dimension=0,
        tiled=True,
    )
    remaining = (rhs.astype(jnp.float32) - removed).astype(jnp.bfloat16)

    def my_rows(solved):
        shaped = solved.reshape(tail_cycles, row_count, block_rows, voxels)
        return lax.dynamic_slice_in_dim(shaped, row_pos, 1, 1)

    window = jnp.concatenate([my_rows(solved_first), my_rows(solved_last)], 0)
    lower_part = jnp.where(col_pos == owner_col, window, remaining[per_col - 2 * tail_cycles :])
    return jnp.concatenate([remaining[: per_col - 2 * tail_cycles], lower_part], 0)


def solution(mesh):
    placed = (P(None, "row", None, None, "col"), P("col", "row", None, "vox"), P())
    return jax.shard_map(
        local, mesh=mesh, in_specs=placed, out_specs=P("col", "row", None, "vox"), check_vma=False
    )
```

profile of v0, /device:TPU:1, one launch (start us, length us, event | category | flops | bytes accessed | tf_op | source)
XLA Modules:
  0.0 951.8 jit_solution(15609546226498273052)
XLA Ops:
  6.5 0.0 all-gather.2.cloned.1.call-start
  6.5 1.5 slice.28
  8.1 0.0 all-gather.2.cloned.1.call-update
  8.1 0.0 all-reduce.3.cloned.1.call-start
  8.2 53.5 %all-gather.2.cloned.1.call-done = bf16[1,16,64,768]{3,2,0,1:T(8,128)(2,1)} async-done(((bf16[1,1,64,768]{3,2,0,1:T(8,128)(2,1)}), bf16[1,16,64,768]{3,2,0,1:T(8,128)(2,1)}) %all-gather.2.cloned.1.call-update) | async-done | bytes 1572880 | tf_op jit(solution)/shard_map/all_gather | solution.py:34
  61.6 1.3 broadcast_select_fusion
  62.9 0.0 all-reduce.3.cloned.1.call-update
  62.9 0.0 reduce-scatter.2.cloned.1.call-start
  63.0 1.4 slice.23
  64.4 75.1 %all-reduce.3.cloned.1.call-done = bf16[1024,768]{1,0:T(8,128)(2,1)} async-done(((bf16[1024,768]{1,0:T(8,128)(2,1)}), bf16[1024,768]{1,0:T(8,128)(2,1)}) %all-reduce.3.cloned.1.call-update) | async-done | bytes 1572880 | tf_op jit(solution)/shard_map/psum | solution.py:9
  139.5 3.9 fusion.6
  143.4 0.0 copy-start
  143.4 0.8 dynamic-slice_bitcast_fusion.1
  144.3 0.3 broadcast_in_dim.9
  144.6 0.0 copy-done
  144.6 0.6 copy-done.3
  145.2 0.0 copy-done.5
  145.2 0.2 fusion.15
  145.5 610.3 %all-reduce.4 = bf16[1,16,64,768]{3,2,1,0:T(8,128)(2,1)} all-reduce(f32[1,16,64,768]{3,2,1,0:T(8,128)S(1)} %fusion.15), channel_id=1, replica_groups=mesh['row'=16,'col'=8,'vox'=2] {'row','col'}, use_global_device_ids=true, to_apply=%region_1.2 | all-reduce | flops 786432 | bytes 4718592 | tf_op jit(solution)/shard_map/psum | solution.py:49
  755.8 4.0 fusion.9
  759.8 0.1 dynamic-slice_bitcast_fusion
  759.9 0.0 copy-done.2
  759.9 0.0 copy-done.4
  759.9 3.7 convolution_bitcast_fusion
  763.6 0.0 reduce-scatter.2.cloned.1.call-update
  763.6 1.4 copy-done.1
  765.0 1.6 copy.26
  766.5 0.7 copy.24
  767.2 0.9 constant_dynamic-slice_fusion
  768.1 175.1 %reduce-scatter.2.cloned.1.call-done = f32[4,1,64,768]{3,2,0,1:T(8,128)} async-done(((f32[32,1,64,768]{3,2,0,1:T(8,128)}), f32[4,1,64,768]{3,2,0,1:T(8,128)}) %reduce-scatter.2.cloned.1.call-update) | async-done | bytes 786448 | tf_op jit(solution)/shard_map/reduce_scatter | solution.py:54
  943.3 1.2 subtract_convert_fusion
  944.5 0.8 maximum_bitcast_fusion.2
  (7 shorter events, 0.1 us)
Async XLA Ops:
  6.5 55.1 %all-gather.2.cloned.1.call-start = ((), (), s32[]{:S(2)}) async-start(), calls=%async_computation.1 | async-start | bytes 1671168 | tf_op jit(solution)/shard_map/all_gather | solution.py:34
  8.1 131.4 %all-reduce.3.cloned.1.call-start = ((), (), s32[]{:S(2)}) async-start(), calls=%async_computation.2 | async-start | bytes 3145728 | tf_op jit(solution)/shard_map/psum | solution.py:9
  62.9 880.4 %reduce-scatter.2.cloned.1.call-start = ((), (), s32[]{:S(2)}) async-start(), calls=%async_computation.3 | async-start | bytes 7077888 | tf_op jit(solution)/shard_map/reduce_scatter | solution.py:54
  143.4 1.2 copy-start
  144.3 1.0 copy-start.3
  144.3 1.0 copy-start.5
  755.8 4.1 copy-start.2
  755.8 4.1 copy-start.4
  763.6 1.4 copy-start.1
Sparse Core Ops, SparseCore 0:
  9.8 51.8 all-gather.1
  64.0 75.4 all-reduce.2
  763.7 179.5 reduce-scatter.1
where the time goes:
time: 952 us
  blocking collectives  610 us (64%)
  waiting for transfers between devices  304 us (32%)
  between operations  13.2 us (1%)
  matrix products  11.8 us (1%)
    psum x1, blocking collectives, local(): middle_rhs = lax.psum(padded, ('row', 'col')).astype(jnp.bfloat16)  610 us
    reduce_scatter x1, waiting for transfers between devices, local(): lax.psum_scatter(jnp.einsum('kprjc,jcv->kprv', coeffs_r, stacked_mine, pr...  175 us
    psum x1, waiting for transfers between devices, spread(): return lax.psum(jnp.where(mine, value, jnp.zeros_like(value)), axis)  75.1 us
    all_gather x1, waiting for transfers between devices, local(): tail_rows = lax.all_gather(tail_piece, 'row', axis=1, tiled=True)  53.5 us
  transfers between devices with their start and end apart: 3, of which 3 were waited for; matrix products, arithmetic and copies ran while one was open for 0% of the time, Pallas kernels for 0%

commit v1 on v0

--- a/solution.py
+++ b/solution.py
@@ -31,7 +31,12 @@
     tail_cycles = block_order // (block_rows * row_count)
     owner_col = col_count - 1
     tail_piece = rhs[per_col - tail_cycles :]
-    tail_rows = lax.all_gather(tail_piece, "row", axis=1, tiled=True)
+    ring = [tail_piece]
+    for hop in range(15):
+        ring.append(lax.ppermute(ring[-1], "row", [(dev, (dev + 1) % 16) for dev in range(16)]))
+    tail_rows = jnp.roll(
+        jnp.concatenate(ring[::-1], axis=1), (lax.axis_index("row") + 1) * ring[0].shape[1], axis=1
+    )
     tail_rows = spread(tail_rows, "col", owner_col)
     solved_last, last_mine = solve_block(
         inverses[1], tail_rows.reshape(block_order, voxels), col_pos, own_cols

time: 952 us -> 1020 us (1.071)
  waiting for transfers between devices: 304 us -> 367 us
    ppermute x0 -> x15, waiting for transfers between devices: none -> 103 us  [local(): lax.ppermute(ring[-1], 'row', [(dev, (dev + 1) % 16) for dev in range(16)])]
    all_gather x1 -> x0, waiting for transfers between devices: 53.5 us -> none  [local(): tail_rows = lax.all_gather(tail_piece, 'row', axis=1, tiled=True)]
    psum x1, waiting for transfers between devices: 75.1 us -> 88.1 us  [spread(): return lax.psum(jnp.where(mine, value, jnp.zeros_like(value)), axis)]
  transfers between devices with their start and end apart: 3 -> 17, of which waited for: 3 -> 17; matrix products, arithmetic and copies ran while one was open for 0% -> 0% of each run, Pallas kernels for 0% -> 0%
where the time goes in v1:
time: 1020 us
  blocking collectives  610 us (60%)
  waiting for transfers between devices  367 us (36%)
  between operations  13.8 us (1%)
  matrix products  11.8 us (1%)
    psum x1, blocking collectives, local(): middle_rhs = lax.psum(padded, ('row', 'col')).astype(jnp.bfloat16)  610 us
    reduce_scatter x1, waiting for transfers between devices, local(): lax.psum_scatter(jnp.einsum('kprjc,jcv->kprv', coeffs_r, stacked_mine, pr...  176 us
    ppermute x15, waiting for transfers between devices, local(): lax.ppermute(ring[-1], 'row', [(dev, (dev + 1) % 16) for dev in range(16)])  103 us
    psum x1, waiting for transfers between devices, spread(): return lax.psum(jnp.where(mine, value, jnp.zeros_like(value)), axis)  88.1 us
  transfers between devices with their start and end apart: 17, of which 17 were waited for; matrix products, arithmetic and copies ran while one was open for 0% of the time, Pallas kernels for 0%

profile of v1, /device:TPU:1, one launch (start us, length us, event | category | flops | bytes accessed | tf_op | source)
XLA Modules:
  0.0 1016.6 jit_solution(17057649622156255049)
XLA Ops:
  6.5 1.0 slice.21
  7.5 2.0 collective-permute-start
  9.5 5.7 collective-permute-done
  15.3 6.8 collective-permute-done.1
  22.1 6.8 collective-permute-done.2
  28.9 6.8 collective-permute-done.3
  35.6 7.2 collective-permute-done.4
  42.9 7.6 collective-permute-done.5
  50.4 6.8 collective-permute-done.6
  57.2 6.8 collective-permute-done.7
  64.0 6.8 collective-permute-done.8
  70.8 6.8 collective-permute-done.9
  77.6 6.8 collective-permute-done.10
  84.4 7.1 collective-permute-done.11
  91.4 7.8 collective-permute-done.12
  99.3 6.8 collective-permute-done.13
  106.1 6.8 collective-permute-done.14
  113.4 1.2 dynamic-slice_select_fusion
  114.9 1.4 slice.23
  116.3 88.1 %all-reduce.3.cloned.1.call-done = bf16[1024,768]{1,0:T(8,128)(2,1)} async-done(((bf16[1024,768]{1,0:T(8,128)(2,1)}), bf16[1024,768]{1,0:T(8,128)(2,1)}) %all-reduce.3.cloned.1.call-update) | async-done | bytes 1572880 | tf_op jit(solution)/shard_map/psum | solution.py:9
  204.3 3.9 fusion.6
  208.3 0.8 dynamic-slice_bitcast_fusion.1
  209.7 609.8 %all-reduce.4 = bf16[1,16,64,768]{3,2,1,0:T(8,128)(2,1)} all-reduce(f32[1,16,64,768]{3,2,1,0:T(8,128)S(1)} %fusion.15), channel_id=1, replica_groups=mesh['row'=16,'col'=8,'vox'=2] {'row','col'}, use_global_device_ids=true, to_apply=%region_1.2 | all-reduce | flops 786432 | bytes 4718592 | tf_op jit(solution)/shard_map/psum | solution.py:54
  819.6 4.0 fusion.9
  823.7 3.7 convolution_bitcast_fusion
  827.4 1.4 copy-done.1
  828.8 1.6 copy.16
  830.3 0.7 copy.14
  831.0 0.9 constant_dynamic-slice_fusion
  831.9 175.8 %reduce-scatter.2.cloned.1.call-done = f32[4,1,64,768]{3,2,0,1:T(8,128)} async-done(((f32[32,1,64,768]{3,2,0,1:T(8,128)}), f32[4,1,64,768]{3,2,0,1:T(8,128)}) %reduce-scatter.2.cloned.1.call-update) | async-done | bytes 786448 | tf_op jit(solution)/shard_map/reduce_scatter | solution.py:59
  1007.8 1.2 subtract_convert_fusion
  1009.0 0.8 maximum_bitcast_fusion.2
  (66 shorter events, 1.3 us)
Async XLA Ops:
  6.5 106.6 %copy-start.3 = (bf16[4,1,64,768]{3,2,1,0:T(8,128)(2,1)S(1)}, bf16[4,1,64,768]{3,2,1,0:T(8,128)(2,1)}, u32[]{:S(2)}) copy-start(bf16[4,1,64,768]{3,2,1,0:T(8,128)(2,1)} %param.4) | copy-start | bytes 1179652
  6.5 197.8 %all-reduce.3.cloned.1.call-start = ((), (), s32[]{:S(2)}) async-start(), calls=%async_computation.1 | async-start | bytes 3145728 | tf_op jit(solution)/shard_map/psum | solution.py:9
  7.5 7.8 collective-permute-start
  15.3 6.8 collective-permute-start.1
  22.1 6.8 collective-permute-start.2
  28.8 6.8 collective-permute-start.3
  35.6 7.2 collective-permute-start.4
  42.9 7.6 collective-permute-start.5
  50.4 6.8 collective-permute-start.6
  57.2 6.8 collective-permute-start.7
  64.0 6.8 collective-permute-start.8
  70.8 6.8 collective-permute-start.9
  77.6 6.8 collective-permute-start.10
  84.4 7.1 collective-permute-start.11
  91.4 7.8 collective-permute-start.12
  99.3 6.8 collective-permute-start.13
  106.1 6.8 collective-permute-start.14
  114.7 893.1 %reduce-scatter.2.cloned.1.call-start = ((), (), s32[]{:S(2)}) async-start(), calls=%async_computation.2 | async-start | bytes 7077888 | tf_op jit(solution)/shard_map/reduce_scatter | solution.py:59
  208.3 1.2 copy-start
  208.3 1.2 copy-start.5
  819.6 4.1 copy-start.2
  819.6 4.1 copy-start.4
  827.4 1.4 copy-start.1
Sparse Core Ops, SparseCore 0:
  114.8 89.5 all-reduce.2
  827.5 180.2 reduce-scatter.1
